TPU v7x, 256 devices: a whole 4x4x8 slice. The times are simulated.
256 devices in a mesh: seq: 8 (over y_hi, x), row: 8 (over z), col: 4 (over y_lo, core).
Axes of the slice: x: 4, y: 4 (y_hi: 2, y_lo: 2; y = y_hi * 2 + y_lo), z: 8, core: 2. Of those that a mesh axis runs over, the one named last changes fastest.
Arguments:
- alignment: int32 [32768, 256], P('seq'), may hold values from 0 to 20, as said below
- cluster_sizes: int32 [32768], P('seq'), may hold values from 1 to 32, as said below
- block_inverse: float32 [128, 128], replicated, may hold values from -12 to 12
Outputs:
- couplings: float32 [5120, 5120], P(('seq', 'row'), 'col')
Inputs may be any that keep to these rules, and one draw needn't show every extreme that they name: `alignment`: the value 20 marks a gap. `cluster_sizes`: every cluster size is a power of two.
All inputs are finite; a program needn't handle non-finite values.
Results may differ from a plain program's by a relative error of at most 0.0003.
Values sent between devices are 32-bit elements; how exact they have to be, the bound alone decides.
A program may use at most 64 MiB of HBM per device.

v0:
```python
import jax
import jax.numpy as jnp
from jax import lax
from jax.sharding import PartitionSpec as P

Q = 20
POS = 256
PANEL = 128
PSEUDOCOUNT = 0.5


def spread(value, axis, source):
    kept = jnp.where(lax.axis_index(axis) == source, value, 0).astype(value.dtype)
    return lax.psum(kept, axis)


def one_hot_states(states):
    levels = lax.broadcasted_iota(jnp.int32, (1, 1, Q), 2)
    matches = (states[:, :, None] == levels).astype(jnp.bfloat16)
    return matches.reshape(states.shape[0], states.shape[1] * Q)


def covariance_block(pair_block, row_margin, col_margin, weight_total, row_start, col_start):
    row_freq = (1.0 - PSEUDOCOUNT) * row_margin / weight_total + PSEUDOCOUNT / Q
    col_freq = (1.0 - PSEUDOCOUNT) * col_margin / weight_total + PSEUDOCOUNT / Q
    shape_rc = pair_block.shape
    row_ids = row_start + lax.broadcasted_iota(jnp.int32, shape_rc, 0)
    col_ids = col_start + lax.broadcasted_iota(jnp.int32, shape_rc, 1)
    same_pos = row_ids // Q == col_ids // Q
    prior = jnp.where(
        same_pos, jnp.where(row_ids == col_ids, PSEUDOCOUNT / Q, 0.0), PSEUDOCOUNT / (Q * Q)
    )
    joint = (1.0 - PSEUDOCOUNT) * pair_block / weight_total + prior
    return joint - row_freq[:, None] * col_freq[None, :]


def accumulate_pairs(row_states, column_sets, span_widths, seq_weight):
    local_seqs = row_states.shape[0]
    block_rows = min(local_seqs, 1024)
    count_blocks = local_seqs // block_rows
    row_width = row_states.shape[1] * Q

    def blocked(states):
        return states.reshape(count_blocks, block_rows, states.shape[1])

    def add_block(running, block_item):
        pair_totals, row_margin, column_margins = running
        row_block, weight_block, column_blocks = block_item
        row_hot = one_hot_states(row_block)
        weighted = row_hot * weight_block[:, None]
        new_pairs = []
        new_margins = []
        for pair_total, margin_total, states_block, span_width in zip(
            pair_totals, column_margins, column_blocks, span_widths
        ):
            column_hot = one_hot_states(states_block)
            new_pairs.append(
                pair_total
                + lax.dot_general(
                    weighted,
                    column_hot,
                    (((0,), (0,)), ((), ())),
                    preferred_element_type=jnp.float32,
                )
            )
            new_margins.append(
                margin_total + jnp.dot(weight_block, column_hot, preferred_element_type=jnp.float32)
            )
        row_margin = row_margin + jnp.dot(weight_block, row_hot, preferred_element_type=jnp.float32)
        return ((tuple(new_pairs), row_margin, tuple(new_margins)), None)

    initial = (
        tuple((jnp.zeros((row_width, span_width), jnp.float32) for span_width in span_widths)),
        jnp.zeros((row_width,), jnp.float32),
        tuple((jnp.zeros((span_width,), jnp.float32) for span_width in span_widths)),
    )
    block_items = (
        blocked(row_states),
        seq_weight.reshape(count_blocks, block_rows),
        tuple((blocked(states) for states in column_sets)),
    )
    result, unused = lax.scan(add_block, initial, block_items)
    return result


def shards(alignment, cluster_sizes, block_inverse):
    seq_count = lax.axis_size("seq")
    row_count = lax.axis_size("row")
    col_count = lax.axis_size("col")
    seq_index = lax.axis_index("seq")
    row_index = lax.axis_index("row")
    col_index = lax.axis_index("col")
    local_seqs = alignment.shape[0]
    row_positions = POS // (seq_count * row_count)
    col_positions = POS // col_count
    block_features = row_positions * Q
    col_features = col_positions * Q
    seq_weight = (1.0 / cluster_sizes.astype(jnp.float32)).astype(jnp.bfloat16)
    grouped = alignment.reshape(local_seqs, seq_count, row_count, row_positions)
    row_states = lax.dynamic_slice_in_dim(grouped, row_index, 1, 2).reshape(
        local_seqs, seq_count * row_positions
    )
    col_states = lax.dynamic_slice_in_dim(alignment, col_index * col_positions, col_positions, 1)
    weight_local = jnp.sum(seq_weight.astype(jnp.float32))
    row_start = (seq_index * row_count + row_index) * block_features
    col_start = col_index * col_features
    pair_totals, row_margin, column_margins = accumulate_pairs(
        row_states, (col_states,), (col_features,), seq_weight
    )
    weight_total, row_margin, col_margin = lax.psum(
        (weight_local, row_margin, column_margins[0]), "seq"
    )
    pair_tile = lax.psum_scatter(pair_totals[0], "seq", scatter_dimension=0, tiled=True)
    own_margin = lax.dynamic_slice_in_dim(row_margin, seq_index * block_features, block_features)
    cov_tile = covariance_block(
        pair_tile, own_margin, col_margin, weight_total, row_start, col_start
    )
    panel_rows = spread(cov_tile[:, :PANEL], "col", 0)
    sym_inverse = 0.5 * (block_inverse + block_inverse.T)
    left_factor = jnp.dot(panel_rows, sym_inverse, precision=lax.Precision.HIGHEST)
    whole_panel = lax.all_gather(panel_rows, ("seq", "row"), axis=0, tiled=True)
    panel_cols = lax.dynamic_slice_in_dim(whole_panel, col_start, col_features, 0)
    update = lax.dot_general(
        left_factor, panel_cols, (((1,), (1,)), ((), ())), precision=lax.Precision.HIGHEST
    )
    return -Q * (cov_tile - update)


def solution(mesh):
    in_specs = (P("seq", None), P("seq"), P())
    out_specs = P(("seq", "row"), "col")
    return jax.shard_map(shards, mesh=mesh, in_specs=in_specs, out_specs=out_specs, check_vma=False)
```

profile of v0, /device:TPU:6, one launch (start us, length us, event | category | flops | bytes accessed | tf_op | source)
XLA Modules:
  0.0 306.2 jit_solution(9124577262664192869)
XLA Ops:
  6.5 5.6 %copy.9 = s32[4096,256]{0,1:T(8,128)} copy(s32[4096,256]{1,0:T(8,128)} %param.5) | data formatting | bytes 8388608 | tf_op args[0]
  12.1 2.2 constant_dynamic-slice_fusion.4
  14.3 0.6 copy.12
  14.9 5.2 %reshape.159 = s32[4096,8,8,4]{0,3,2,1:T(4,128)} reshape(s32[4096,256]{0,1:T(8,128)} %copy.9) | data formatting | bytes 8388608 | tf_op jit(solution)/shard_map/reshape | solution.py:99
  20.1 1.1 constant_dynamic-slice_fusion.5
  21.2 1.2 reshape_reshape.3
  22.5 0.7 convert_reduce_fusion
  23.1 51.7 %while.15 = (s32[]{:T(128)}, f32[640,1280]{1,0:T(8,128)}, f32[640]{0:T(1024)S(1)}, f32[1280]{0:T(1024)S(1)}, s32[4,1024,32]{1,0,2:T(4,128)}, /*index=5*/bf16[4,1...) while((s32[]{:T(128)}, f32[640,1280]{1,0:T(8,128)}, f32[640]{0:T(1024)S(1)}, ...), condition=%wide.region_1.2_spmd.clone, body=%wide.region_0.0_spmd.clone.sunk | while | flops 1686572800 | bytes 30978228 | solution.py:82
  23.2 1.5 constant_dynamic-slice_fusion.7
  24.8 0.5 broadcast_select_fusion.2
  25.2 1.2 mul.117
  26.5 0.9 iota_compare_fusion.4
  27.4 0.7 eq.120
  28.2 5.0 %convolution_add_fusion.2 = f32[640,1280]{1,0:T(8,128)} fusion(bf16[1024,640]{0,1:T(8,128)(2,1)} %mul.117, pred[1024,1280]{0,1:T(32,128)(4,1)S(1)} %eq.120, f32[640,1280]{1,0:T(8,128)} %get-tuple-element.161, pred[]{:T(512)S(6)} %compare.3), kind=kOutput, calls=%fused_computation.1.clone.1 | convolution fusion | flops 1679360000 | bytes 9175041 | tf_op jit(solution)/shard_map/while/body/eval_jaxpr/dot_general | solution.py:59
  33.2 0.8 convolution_reduce_fusion.5
  34.0 0.4 iota_compare_fusion.5
  34.4 0.4 eq.121
  34.8 0.5 convolution_reduce_fusion.4
  35.3 0.0 copy-done.1
  35.4 1.5 constant_dynamic-slice_fusion.7
  36.9 0.5 broadcast_select_fusion.2
  37.4 1.2 mul.117
  38.7 0.9 iota_compare_fusion.4
  39.6 0.7 eq.120
  40.3 6.0 %convolution_add_fusion.2 = f32[640,1280]{1,0:T(8,128)} fusion(bf16[1024,640]{0,1:T(8,128)(2,1)} %mul.117, pred[1024,1280]{0,1:T(32,128)(4,1)S(1)} %eq.120, f32[640,1280]{1,0:T(8,128)} %get-tuple-element.161, pred[]{:T(512)S(6)} %compare.3), kind=kOutput, calls=%fused_computation.1.clone.1 | convolution fusion | flops 1679360000 | bytes 9175041 | tf_op jit(solution)/shard_map/while/body/eval_jaxpr/dot_general | solution.py:59
  46.4 0.8 convolution_reduce_fusion.5
  47.2 0.4 iota_compare_fusion.5
  47.6 0.4 eq.121
  48.0 0.5 convolution_reduce_fusion.4
  48.5 1.5 constant_dynamic-slice_fusion.7
  50.1 0.5 broadcast_select_fusion.2
  50.6 1.2 mul.117
  51.8 0.9 iota_compare_fusion.4
  52.8 0.7 eq.120
  53.5 6.0 %convolution_add_fusion.2 = f32[640,1280]{1,0:T(8,128)} fusion(bf16[1024,640]{0,1:T(8,128)(2,1)} %mul.117, pred[1024,1280]{0,1:T(32,128)(4,1)S(1)} %eq.120, f32[640,1280]{1,0:T(8,128)} %get-tuple-element.161, pred[]{:T(512)S(6)} %compare.3), kind=kOutput, calls=%fused_computation.1.clone.1 | convolution fusion | flops 1679360000 | bytes 9175041 | tf_op jit(solution)/shard_map/while/body/eval_jaxpr/dot_general | solution.py:59
  59.6 0.8 convolution_reduce_fusion.5
  60.4 0.4 iota_compare_fusion.5
  60.8 0.4 eq.121
  61.2 0.5 convolution_reduce_fusion.4
  61.7 0.0 copy-done.1
  61.7 1.5 constant_dynamic-slice_fusion.7
  63.3 0.5 broadcast_select_fusion.2
  63.8 1.2 mul.117
  65.0 0.9 iota_compare_fusion.4
  66.0 0.7 eq.120
  66.7 6.0 %convolution_add_fusion.2 = f32[640,1280]{1,0:T(8,128)} fusion(bf16[1024,640]{0,1:T(8,128)(2,1)} %mul.117, pred[1024,1280]{0,1:T(32,128)(4,1)S(1)} %eq.120, f32[640,1280]{1,0:T(8,128)} %get-tuple-element.161, pred[]{:T(512)S(6)} %compare.3), kind=kOutput, calls=%fused_computation.1.clone.1 | convolution fusion | flops 1679360000 | bytes 9175041 | tf_op jit(solution)/shard_map/while/body/eval_jaxpr/dot_general | solution.py:59
  72.8 0.8 convolution_reduce_fusion.5
  73.6 0.4 iota_compare_fusion.5
  74.0 0.4 eq.121
  74.4 0.5 convolution_reduce_fusion.4
  74.9 0.0 copy-start.2
  74.9 0.0 reduce-scatter.2.cloned.1.call-update
  74.9 0.0 all-gather.2.cloned.1.call-start
  75.0 36.3 %all-reduce = (f32[1280]{0:T(1024)S(1)}, f32[]{:T(128)}, f32[640]{0:T(1024)S(1)}) all-reduce(f32[1280]{0:T(1024)S(1)} %get-tuple-element.46, f32[]{:T(128)} %get-tuple-element.102, f32[640]{0:T(1024)S(1)} %get-tuple-element.45), channel_id=1, replica_groups=mesh['seq'=8,'row'=8,'col'=4] {'seq'}, use_global_device_ids=true, to_apply=%region_6.7 | all-reduce | flops 1921 | bytes 15368 | tf_op jit(solution)/shard_map/psum | solution.py:110
  111.3 0.7 divide_add_fusion.1
  112.1 0.7 divide_add_fusion
  112.7 51.2 %reduce-scatter.2.cloned.1.call-done = f32[80,1280]{1,0:T(8,128)} async-done(((f32[640,1280]{1,0:T(8,128)}), f32[80,1280]{1,0:T(8,128)}) %reduce-scatter.2.cloned.1.call-update) | async-done | bytes 409616 | tf_op jit(solution)/shard_map/reduce_scatter | solution.py:113
  163.9 1.8 multiply_subtract_fusion
  165.8 11.4 %psum.31 = f32[80,128]{1,0:T(8,128)} all-reduce(f32[80,128]{1,0:T(8,128)S(1)} %slice_select_fusion), channel_id=1, replica_groups=mesh['seq'=8,'row'=8,'col'=4] {'col'}, use_global_device_ids=true, to_apply=%region_7.8 | all-reduce | flops 10240 | bytes 81920 | tf_op jit(solution)/shard_map/psum | solution.py:14
  177.2 0.0 all-gather.2.cloned.1.call-update
  177.2 0.1 copy.13
  177.3 1.0 fusion.6
  178.3 118.5 %all-gather.2.cloned.1.call-done = f32[5120,128]{1,0:T(8,128)} async-done(((f32[80,128]{1,0:T(8,128)}), f32[5120,128]{1,0:T(8,128)}) %all-gather.2.cloned.1.call-update) | async-done | bytes 2621456 | tf_op jit(solution)/shard_map/all_gather | solution.py:121
  296.8 2.6 fusion.3
  (49 shorter events, 0.5 us)
Async XLA Ops:
  6.5 157.4 %reduce-scatter.2.cloned.1.call-start = ((), (), s32[]{:S(2)}) async-start(), calls=%async_computation.1 | async-start | bytes 3686400 | tf_op jit(solution)/shard_map/reduce_scatter | solution.py:113
  20.1 2.3 copy-start.3
  23.1 3.3 %copy-start = (s32[4,1024,64]{1,2,0:T(8,128)}, s32[4,1024,64]{1,2,0:T(8,128)S(1)}, u32[]{:S(2)}) copy-start(s32[4,1024,64]{1,2,0:T(8,128)S(1)} %get-tuple-element.175) | copy-start | bytes 3145732 | tf_op jit(solution)/shard_map/while
  33.2 2.1 copy-start.1
  35.3 3.3 %copy-start = (s32[4,1024,64]{1,2,0:T(8,128)}, s32[4,1024,64]{1,2,0:T(8,128)S(1)}, u32[]{:S(2)}) copy-start(s32[4,1024,64]{1,2,0:T(8,128)S(1)} %get-tuple-element.175) | copy-start | bytes 3145732 | tf_op jit(solution)/shard_map/while
  46.4 2.1 copy-start.1
  48.5 3.3 %copy-start = (s32[4,1024,64]{1,2,0:T(8,128)}, s32[4,1024,64]{1,2,0:T(8,128)S(1)}, u32[]{:S(2)}) copy-start(s32[4,1024,64]{1,2,0:T(8,128)S(1)} %get-tuple-element.175) | copy-start | bytes 3145732 | tf_op jit(solution)/shard_map/while
  59.6 2.1 copy-start.1
  61.7 3.3 %copy-start = (s32[4,1024,64]{1,2,0:T(8,128)}, s32[4,1024,64]{1,2,0:T(8,128)S(1)}, u32[]{:S(2)}) copy-start(s32[4,1024,64]{1,2,0:T(8,128)S(1)} %get-tuple-element.175) | copy-start | bytes 3145732 | tf_op jit(solution)/shard_map/while
  72.8 2.1 copy-start.1
  74.9 102.3 %copy-start.2 = (f32[128,128]{1,0:T(8,128)S(1)}, f32[128,128]{1,0:T(8,128)}, u32[]{:S(2)}) copy-start(f32[128,128]{1,0:T(8,128)} %param.7) | copy-start | bytes 196612
  74.9 221.8 %all-gather.2.cloned.1.call-start = ((), (), s32[]{:S(2)}) async-start(), calls=%async_computation.2 | async-start | bytes 2662400 | tf_op jit(solution)/shard_map/all_gather | solution.py:121
Sparse Core Ops, SparseCore 0:
  75.0 88.8 reduce-scatter.1
  177.3 119.4 all-gather.1
where the time goes:
time: 307 us; the launch traced here: 306 us
  waiting for transfers between devices  170 us (55%)
  blocking collectives  47.6 us (16%)
  matrix products  31.8 us (10%)
  local copies, waits for them, and re-layouts  31.7 us (10%)
  between operations  13.5 us (4%)
  other arithmetic  11.4 us (4%)
    all_gather x1, waiting for transfers between devices, shards(): whole_panel = lax.all_gather(panel_rows, ('seq', 'row'), axis=0, tiled=True)  118 us
    reduce_scatter x1, waiting for transfers between devices, shards(): lax.psum_scatter(pair_totals[0], 'seq', scatter_dimension=0, tiled=True)  51.2 us
    psum x1, blocking collectives, shards(): lax.psum((weight_local, row_margin, column_margins[0]), 'seq')  36.3 us
    dot_general x4, matrix products, add_block(): lax.dot_general(weighted, column_hot, (((0,), (0,)), ((), ())), preferred...  23.1 us
    psum x1, blocking collectives, spread(): return lax.psum(kept, axis)  11.4 us
    dynamic_slice x12, local copies, waits for them, and re-layouts, accumulate_pairs(): result, unused = lax.scan(add_block, initial, block_items)  6.38 us
    unnamed x7, local copies, waits for them, and re-layouts  6.29 us
  transfers between devices with their start and end apart: 2, of which 2 were waited for; matrix products, arithmetic and copies ran while one was open for 1% of the time, Pallas kernels for 0%

commit v1 on v0

--- a/solution.py
+++ b/solution.py
@@ -118,7 +118,12 @@
     panel_rows = spread(cov_tile[:, :PANEL], "col", 0)
     sym_inverse = 0.5 * (block_inverse + block_inverse.T)
     left_factor = jnp.dot(panel_rows, sym_inverse, precision=lax.Precision.HIGHEST)
-    whole_panel = lax.all_gather(panel_rows, ("seq", "row"), axis=0, tiled=True)
+    whole_panel = jnp.concatenate(
+        lax.all_to_all(
+            jnp.stack([panel_rows] * lax.axis_size(("seq", "row"))), ("seq", "row"), 0, 0
+        ),
+        axis=0,
+    )
     panel_cols = lax.dynamic_slice_in_dim(whole_panel, col_start, col_features, 0)
     update = lax.dot_general(
         left_factor, panel_cols, (((1,), (1,)), ((), ())), precision=lax.Precision.HIGHEST

time: 307 us -> 262 us (0.85)
  waiting for transfers between devices: 170 us -> 114 us
  starting transfers between devices: 0.04 us -> 10.4 us
    all_gather x1 -> x0, waiting for transfers between devices: 118 us -> none  [shards(): whole_panel = lax.all_gather(panel_rows, ('seq', 'row'), axis=0, tiled=True)]
    all_to_all x0 -> x1, waiting for transfers between devices: none -> 62.6 us  [shards(): lax.all_to_all(jnp.stack([panel_rows] * lax.axis_size(('seq', 'row'))), (...]
    all_to_all x0 -> x1, starting transfers between devices: none -> 10.4 us  [shards(): lax.all_to_all(jnp.stack([panel_rows] * lax.axis_size(('seq', 'row'))), (...]
where the time goes in v1:
time: 262 us; the launch traced here: 260 us
  waiting for transfers between devices  114 us (44%)
  blocking collectives  47.1 us (18%)
  local copies, waits for them, and re-layouts  33.4 us (13%)
  matrix products  29.9 us (11%)
  between operations  13.5 us (5%)
  other arithmetic  11.4 us (4%)
  starting transfers between devices  10.4 us (4%)
    all_to_all x1, waiting for transfers between devices, shards(): lax.all_to_all(jnp.stack([panel_rows] * lax.axis_size(('seq', 'row'))), (...  62.6 us
    reduce_scatter x1, waiting for transfers between devices, shards(): lax.psum_scatter(pair_totals[0], 'seq', scatter_dimension=0, tiled=True)  51.2 us
    psum x1, blocking collectives, shards(): lax.psum((weight_local, row_margin, column_margins[0]), 'seq')  36.3 us
    dot_general x4, matrix products, add_block(): lax.dot_general(weighted, column_hot, (((0,), (0,)), ((), ())), preferred...  23.1 us
    psum x1, blocking collectives, spread(): return lax.psum(kept, axis)  10.8 us
    all_to_all x1, starting transfers between devices, shards(): lax.all_to_all(jnp.stack([panel_rows] * lax.axis_size(('seq', 'row'))), (...  10.4 us
    dynamic_slice x12, local copies, waits for them, and re-layouts, accumulate_pairs(): result, unused = lax.scan(add_block, initial, block_items)  6.38 us
    unnamed x7, local copies, waits for them, and re-layouts  6.29 us
  transfers between devices with their start and end apart: 2, of which 2 were waited for; matrix products, arithmetic and copies ran while one was open for 1% of the time, Pallas kernels for 0%

profile of v1, /device:TPU:6, one launch (start us, length us, event | category | flops | bytes accessed | tf_op | source)
XLA Modules:
  0.0 260.0 jit_solution(16580192273080622342)
XLA Ops:
  6.5 5.6 %copy.9 = s32[4096,256]{0,1:T(8,128)} copy(s32[4096,256]{1,0:T(8,128)} %param.5) | data formatting | bytes 8388608 | tf_op args[0]
  12.1 2.2 constant_dynamic-slice_fusion.4
  14.3 0.6 copy.12
  14.9 0.0 copy-start.3
  15.0 5.2 %reshape.164 = s32[4096,8,8,4]{0,3,2,1:T(4,128)} reshape(s32[4096,256]{0,1:T(8,128)} %copy.9) | data formatting | bytes 8388608 | tf_op jit(solution)/shard_map/reshape | solution.py:99
  20.1 1.1 constant_dynamic-slice_fusion.5
  21.2 1.2 reshape_reshape.3
  22.5 0.7 convert_reduce_fusion
  23.1 51.7 %while.15 = (s32[]{:T(128)}, f32[640,1280]{1,0:T(8,128)}, f32[640]{0:T(1024)S(1)}, f32[1280]{0:T(1024)S(1)}, s32[4,1024,32]{1,0,2:T(4,128)}, /*index=5*/bf16[4,1...) while((s32[]{:T(128)}, f32[640,1280]{1,0:T(8,128)}, f32[640]{0:T(1024)S(1)}, ...), condition=%wide.region_1.2_spmd.clone, body=%wide.region_0.0_spmd.clone.sunk | while | flops 1686572800 | bytes 30978228 | solution.py:82
  23.2 1.5 constant_dynamic-slice_fusion.7
  24.8 0.5 broadcast_select_fusion.2
  25.2 1.2 mul.117
  26.5 0.0 copy-done
  26.5 0.9 iota_compare_fusion.4
  27.4 0.7 eq.120
  28.2 5.0 %convolution_add_fusion.2 = f32[640,1280]{1,0:T(8,128)} fusion(bf16[1024,640]{0,1:T(8,128)(2,1)} %mul.117, pred[1024,1280]{0,1:T(32,128)(4,1)S(1)} %eq.120, f32[640,1280]{1,0:T(8,128)} %get-tuple-element.161, pred[]{:T(512)S(6)} %compare.3), kind=kOutput, calls=%fused_computation.1.clone.1 | convolution fusion | flops 1679360000 | bytes 9175041 | tf_op jit(solution)/shard_map/while/body/eval_jaxpr/dot_general | solution.py:59
  33.2 0.8 convolution_reduce_fusion.5
  34.0 0.4 iota_compare_fusion.5
  34.4 0.4 eq.121
  34.8 0.5 convolution_reduce_fusion.4
  35.3 0.0 copy-done.1
  35.4 1.5 constant_dynamic-slice_fusion.7
  36.9 0.5 broadcast_select_fusion.2
  37.4 1.2 mul.117
  38.7 0.9 iota_compare_fusion.4
  39.6 0.7 eq.120
  40.3 6.0 %convolution_add_fusion.2 = f32[640,1280]{1,0:T(8,128)} fusion(bf16[1024,640]{0,1:T(8,128)(2,1)} %mul.117, pred[1024,1280]{0,1:T(32,128)(4,1)S(1)} %eq.120, f32[640,1280]{1,0:T(8,128)} %get-tuple-element.161, pred[]{:T(512)S(6)} %compare.3), kind=kOutput, calls=%fused_computation.1.clone.1 | convolution fusion | flops 1679360000 | bytes 9175041 | tf_op jit(solution)/shard_map/while/body/eval_jaxpr/dot_general | solution.py:59
  46.4 0.8 convolution_reduce_fusion.5
  47.2 0.4 iota_compare_fusion.5
  47.6 0.4 eq.121
  48.0 0.5 convolution_reduce_fusion.4
  48.5 1.5 constant_dynamic-slice_fusion.7
  50.1 0.5 broadcast_select_fusion.2
  50.6 1.2 mul.117
  51.8 0.9 iota_compare_fusion.4
  52.8 0.7 eq.120
  53.5 6.0 %convolution_add_fusion.2 = f32[640,1280]{1,0:T(8,128)} fusion(bf16[1024,640]{0,1:T(8,128)(2,1)} %mul.117, pred[1024,1280]{0,1:T(32,128)(4,1)S(1)} %eq.120, f32[640,1280]{1,0:T(8,128)} %get-tuple-element.161, pred[]{:T(512)S(6)} %compare.3), kind=kOutput, calls=%fused_computation.1.clone.1 | convolution fusion | flops 1679360000 | bytes 9175041 | tf_op jit(solution)/shard_map/while/body/eval_jaxpr/dot_general | solution.py:59
  59.6 0.8 convolution_reduce_fusion.5
  60.4 0.4 iota_compare_fusion.5
  60.8 0.4 eq.121
  61.2 0.5 convolution_reduce_fusion.4
  61.7 1.5 constant_dynamic-slice_fusion.7
  63.3 0.5 broadcast_select_fusion.2
  63.8 1.2 mul.117
  65.0 0.9 iota_compare_fusion.4
  66.0 0.7 eq.120
  66.7 6.0 %convolution_add_fusion.2 = f32[640,1280]{1,0:T(8,128)} fusion(bf16[1024,640]{0,1:T(8,128)(2,1)} %mul.117, pred[1024,1280]{0,1:T(32,128)(4,1)S(1)} %eq.120, f32[640,1280]{1,0:T(8,128)} %get-tuple-element.161, pred[]{:T(512)S(6)} %compare.3), kind=kOutput, calls=%fused_computation.1.clone.1 | convolution fusion | flops 1679360000 | bytes 9175041 | tf_op jit(solution)/shard_map/while/body/eval_jaxpr/dot_general | solution.py:59
  72.8 0.8 convolution_reduce_fusion.5
  73.6 0.4 iota_compare_fusion.5
  74.0 0.4 eq.121
  74.4 0.5 convolution_reduce_fusion.4
  74.9 0.0 reduce-scatter.2.cloned.1.call-update
  74.9 36.3 %all-reduce = (f32[1280]{0:T(1024)S(1)}, f32[]{:T(128)}, f32[640]{0:T(1024)S(1)}) all-reduce(f32[1280]{0:T(1024)S(1)} %get-tuple-element.46, f32[]{:T(128)} %get-tuple-element.102, f32[640]{0:T(1024)S(1)} %get-tuple-element.45), channel_id=1, replica_groups=mesh['seq'=8,'row'=8,'col'=4] {'seq'}, use_global_device_ids=true, to_apply=%region_6.7 | all-reduce | flops 1921 | bytes 15368 | tf_op jit(solution)/shard_map/psum | solution.py:110
  111.3 0.7 divide_add_fusion.1
  112.0 0.7 divide_add_fusion
  112.7 51.2 %reduce-scatter.2.cloned.1.call-done = f32[80,1280]{1,0:T(8,128)} async-done(((f32[640,1280]{1,0:T(8,128)}), f32[80,1280]{1,0:T(8,128)}) %reduce-scatter.2.cloned.1.call-update) | async-done | bytes 409616 | tf_op jit(solution)/shard_map/reduce_scatter | solution.py:113
  163.9 1.8 multiply_subtract_fusion
  165.8 10.8 %psum.31 = f32[80,128]{1,0:T(8,128)S(1)} all-reduce(f32[80,128]{1,0:T(8,128)S(1)} %slice_select_fusion), channel_id=1, replica_groups=mesh['seq'=8,'row'=8,'col'=4] {'col'}, use_global_device_ids=true, to_apply=%region_7.8 | all-reduce | flops 10240 | bytes 81920 | tf_op jit(solution)/shard_map/psum | solution.py:14
  176.6 1.7 stack.2
  178.2 10.4 %all-to-all-start = ((f32[64,80,128]{2,1,0:T(8,128)}), f32[64,80,128]{2,1,0:T(8,128)S(1)}, u32[]{:S(2)}, u32[]{:S(2)}) async-start(f32[64,80,128]{2,1,0:T(8,128)} %stack.2), calls=%async_computation.1 | async-start | bytes 5242880 | tf_op jit(solution)/shard_map/all_to_all | solution.py:122
  188.7 0.1 copy.13
  188.8 0.2 fusion.6
  189.0 62.6 %all-to-all-done = f32[64,80,128]{2,1,0:T(8,128)S(1)} async-done(((f32[64,80,128]{2,1,0:T(8,128)}), f32[64,80,128]{2,1,0:T(8,128)S(1)}, u32[]{:S(2)}, u32[]{:S(2)}) %all-to-all-start) | async-done | bytes 2621472 | tf_op jit(solution)/shard_map/all_to_all | solution.py:122
  251.6 1.6 fusion.3
  (49 shorter events, 0.5 us)
Async XLA Ops:
  6.5 157.4 %reduce-scatter.2.cloned.1.call-start = ((), (), s32[]{:S(2)}) async-start(), calls=%async_computation.2 | async-start | bytes 3686400 | tf_op jit(solution)/shard_map/reduce_scatter | solution.py:113
  14.9 7.5 %copy-start.3 = (s32[4096]{0:T(1024)S(1)}, s32[4096]{0:T(1024)}, u32[]{:S(2)}) copy-start(s32[4096]{0:T(1024)} %param.6) | copy-start | bytes 49156
  23.1 3.3 %copy-start = (s32[4,1024,64]{1,2,0:T(8,128)}, s32[4,1024,64]{1,2,0:T(8,128)S(1)}, u32[]{:S(2)}) copy-start(s32[4,1024,64]{1,2,0:T(8,128)S(1)} %get-tuple-element.175) | copy-start | bytes 3145732 | tf_op jit(solution)/shard_map/while
  33.2 2.1 copy-start.1
  35.3 3.3 %copy-start = (s32[4,1024,64]{1,2,0:T(8,128)}, s32[4,1024,64]{1,2,0:T(8,128)S(1)}, u32[]{:S(2)}) copy-start(s32[4,1024,64]{1,2,0:T(8,128)S(1)} %get-tuple-element.175) | copy-start | bytes 3145732 | tf_op jit(solution)/shard_map/while
  46.4 2.1 copy-start.1
  48.5 3.3 %copy-start = (s32[4,1024,64]{1,2,0:T(8,128)}, s32[4,1024,64]{1,2,0:T(8,128)S(1)}, u32[]{:S(2)}) copy-start(s32[4,1024,64]{1,2,0:T(8,128)S(1)} %get-tuple-element.175) | copy-start | bytes 3145732 | tf_op jit(solution)/shard_map/while
  59.6 2.1 copy-start.1
  61.7 3.3 %copy-start = (s32[4,1024,64]{1,2,0:T(8,128)}, s32[4,1024,64]{1,2,0:T(8,128)S(1)}, u32[]{:S(2)}) copy-start(s32[4,1024,64]{1,2,0:T(8,128)S(1)} %get-tuple-element.175) | copy-start | bytes 3145732 | tf_op jit(solution)/shard_map/while
  72.8 2.1 copy-start.1
  178.2 10.4 %copy-start.2 = (f32[128,128]{1,0:T(8,128)S(1)}, f32[128,128]{1,0:T(8,128)}, u32[]{:S(2)}) copy-start(f32[128,128]{1,0:T(8,128)} %param.7) | copy-start | bytes 196612
  178.2 73.4 %all-to-all-start = ((f32[64,80,128]{2,1,0:T(8,128)}), f32[64,80,128]{2,1,0:T(8,128)S(1)}, u32[]{:S(2)}, u32[]{:S(2)}) async-start(f32[64,80,128]{2,1,0:T(8,128)} %stack.2), calls=%async_computation.1 | async-start | bytes 5242880 | tf_op jit(solution)/shard_map/all_to_all | solution.py:122
Sparse Core Ops, SparseCore 0:
  75.0 88.8 reduce-scatter.1
